TPU v7x, 512 devices: a whole 4x4x16 slice. The times are simulated.
512 devices in a mesh: dp: 512 (over x, z, y, core).
Axes of the slice: x: 4, y: 4, z: 16, core: 2. Of those that a mesh axis runs over, the one named last changes fastest.
Arguments:
- image: bfloat16 [196608, 1152], P('dp'), may hold values from -2 to 2
- text: bfloat16 [196608, 1152], P('dp'), may hold values from -2 to 2
- text_in: bfloat16 [196608, 576], P('dp'), may hold values from -0.015625 to 0.015625
- log_scale: float32 [1], replicated, may hold values from 1.5 to 2.5
- bias: float32 [1], replicated, may hold values from -4 to -1
Outputs:
- image_grad: bfloat16 [196608, 1152], P('dp')
- text_grad: bfloat16 [196608, 1152], P('dp')
- head_grad: bfloat16 [576, 576], replicated
All inputs are finite; a program needn't handle non-finite values.
Results may differ from a plain program's by a relative error of at most 0.0065.
Values may be sent and summed in bfloat16 or wider, within the bound.
A program may use at most 64 MiB of HBM per device.

v0:
```python
import jax
import jax.numpy as jnp
from jax import lax
from jax.sharding import PartitionSpec as P

HOUT = 576
REACH = 2


EPS = 1e-06


def shifted(value, axis, steps):
    count = lax.axis_size(axis)
    pairs = [(source, (source + steps) % count) for source in range(count)]
    return lax.ppermute(value, axis, pairs)


def unit_rows(values):
    wide = values.astype(jnp.float32)
    inverse = lax.rsqrt(jnp.sum(wide * wide, axis=-1, keepdims=True) + EPS)
    return (wide * inverse, inverse)


def pair_tile(left, right, logit_scale, logit_bias, diagonal):
    logits = (
        logit_scale
        * lax.dot_general(left, right, (((1,), (1,)), ((), ())), preferred_element_type=jnp.float32)
        + logit_bias
    )
    tile_grad = jax.nn.sigmoid(logits)
    if diagonal:
        tile_grad = tile_grad - jnp.eye(left.shape[0], dtype=jnp.float32)
    return tile_grad.astype(jnp.bfloat16)


def column_sums(tile_grad, rows_low):
    return lax.dot_general(
        tile_grad, rows_low, (((0,), (0,)), ((), ())), preferred_element_type=jnp.float32
    )


def per_device(image, text, text_in, log_scale, bias):
    logit_scale = jnp.exp(log_scale[0])
    logit_bias = bias[0]
    unit_img, inv_img = unit_rows(image)
    unit_txt, inv_txt = unit_rows(text)
    img_low = unit_img.astype(jnp.bfloat16)
    txt_low = unit_txt.astype(jnp.bfloat16)
    own_tile = pair_tile(img_low, txt_low, logit_scale, logit_bias, True)
    grad_img = jnp.dot(own_tile, txt_low, preferred_element_type=jnp.float32)
    grad_txt = column_sums(own_tile, img_low)
    payload = jnp.stack([txt_low, img_low])
    upper_block = payload
    lower_block = payload
    upper_parts = []
    lower_parts = []
    for distance in range(REACH):
        upper_block = shifted(upper_block, "dp", -1)
        lower_block = shifted(lower_block, "dp", 1)
        for nearby, pieces in ((upper_block, upper_parts), (lower_block, lower_parts)):
            tile_grad = pair_tile(img_low, nearby[0], logit_scale, logit_bias, False)
            grad_img = grad_img + jnp.dot(tile_grad, nearby[0], preferred_element_type=jnp.float32)
            back_tile = pair_tile(nearby[1], txt_low, logit_scale, logit_bias, False)
            grad_txt = grad_txt + column_sums(back_tile, nearby[1])
    grad_img = logit_scale * grad_img
    grad_txt = logit_scale * grad_txt
    image_grad = (
        (grad_img - unit_img * jnp.sum(unit_img * grad_img, axis=-1, keepdims=True)) * inv_img
    ).astype(jnp.bfloat16)
    text_grad = (
        (grad_txt - unit_txt * jnp.sum(unit_txt * grad_txt, axis=-1, keepdims=True)) * inv_txt
    ).astype(jnp.bfloat16)
    head_term = lax.dot_general(
        text_in, text_grad[:, :HOUT], (((0,), (0,)), ((), ())), preferred_element_type=jnp.float32
    )
    head_grad = lax.psum(head_term, "dp").astype(jnp.bfloat16)
    return (image_grad, text_grad, head_grad)


def solution(mesh):
    placed = (P("dp", None), P("dp", None), P("dp", None), P(), P())
    return jax.shard_map(
        per_device,
        mesh=mesh,
        in_specs=placed,
        out_specs=(P("dp", None), P("dp", None), P()),
        check_vma=False,
    )
```

profile of v0, /device:TPU:1, one launch (start us, length us, event | category | flops | bytes accessed | tf_op | source)
XLA Modules:
  0.0 205.1 jit_solution(13094286223629237415)
XLA Ops:
  0.7 1.6 fusion.14
  2.2 1.4 fusion.19
  3.7 0.4 fusion.120
  4.2 4.6 %collective-permute-start.1 = (bf16[2,384,1152]{2,1,0:T(8,128)(2,1)S(1)}, bf16[2,384,1152]{2,1,0:T(8,128)(2,1)}, u32[]{:S(2)}, u32[]{:S(2)}) collective-permute-start(bf16[2,384,1152]{2,1,0:T(8,128)(2,1)S(1)} %pad_maximum_fusion), channel_id=1, source_target_pairs={{0,1},{1,2},{2,3},{3,4},{4,5},{5,6},{6,7},{7,8},{8,9},{9,10},{10,1... | collective-permute-start | bytes 5308424 | tf_op jit(solution)/shard_map/ppermute | solution.py:16
  8.9 6.1 %collective-permute-start = (bf16[2,384,1152]{2,1,0:T(8,128)(2,1)S(1)}, bf16[2,384,1152]{2,1,0:T(8,128)(2,1)}, u32[]{:S(2)}, u32[]{:S(2)}) collective-permute-start(bf16[2,384,1152]{2,1,0:T(8,128)(2,1)S(1)} %pad_maximum_fusion), channel_id=1, source_target_pairs={{0,511},{1,0},{2,1},{3,2},{4,3},{5,4},{6,5},{7,6},{8,7},{9,8},{10,... | collective-permute-start | bytes 5308424 | tf_op jit(solution)/shard_map/ppermute | solution.py:16
  16.3 0.8 fusion.66
  17.1 2.0 fusion.131
  19.1 9.2 %collective-permute-done.1 = bf16[2,384,1152]{2,1,0:T(8,128)(2,1)} collective-permute-done((bf16[2,384,1152]{2,1,0:T(8,128)(2,1)S(1)}, bf16[2,384,1152]{2,1,0:T(8,128)(2,1)}, u32[]{:S(2)}, u32[]{:S(2)}) %collective-permute-start.1) | collective-permute-done | bytes 1769504 | tf_op jit(solution)/shard_map/ppermute | solution.py:16
  28.3 4.5 %collective-permute-start.3 = (bf16[2,384,1152]{2,1,0:T(8,128)(2,1)}, bf16[2,384,1152]{2,1,0:T(8,128)(2,1)}, u32[]{:S(2)}, u32[]{:S(2)}) collective-permute-start(bf16[2,384,1152]{2,1,0:T(8,128)(2,1)} %collective-permute-done.1), channel_id=1, source_target_pairs={{0,1},{1,2},{2,3},{3,4},{4,5},{5,6},{6,7},{7,8},{8,9},{9,10},{10,1... | collective-permute-start | bytes 5308424 | tf_op jit(solution)/shard_map/ppermute | solution.py:16
  32.8 2.0 fusion.110
  34.8 12.6 %collective-permute-start.2 = (bf16[2,384,1152]{2,1,0:T(8,128)(2,1)}, bf16[2,384,1152]{2,1,0:T(8,128)(2,1)}, u32[]{:S(2)}, u32[]{:S(2)}) collective-permute-start(bf16[2,384,1152]{2,1,0:T(8,128)(2,1)} %collective-permute-done), channel_id=1, source_target_pairs={{0,511},{1,0},{2,1},{3,2},{4,3},{5,4},{6,5},{7,6},{8,7},{9,8},{10,... | collective-permute-start | bytes 5308424 | tf_op jit(solution)/shard_map/ppermute | solution.py:16
  47.4 4.6 %convolution_add_fusion.5 = f32[384,1152]{1,0:T(8,128)} fusion(f32[384,1152]{1,0:T(8,128)} %fusion.131, bf16[2,384,1152]{2,1,0:T(8,128)(2,1)} %collective-permute-done, f32[]{:T(128)} %bitcast.59, f32[]{:T(128)} %bitcast, bf16[384,1152]{1,0:T(8,128)(2,1)S(1)} %copy-done.2, f32[384]{0:T(512)S(1)} %add_rsqrt_fusion.1), kind=kOutput, calls=%fused_computation.9 | convolution fusion | flops 682131456 | bytes 6194696 | tf_op jit(solution)/shard_map/dot_general | solution.py:63
  52.0 4.6 %convolution_add_fusion.4 = f32[384,1152]{1,0:T(8,128)} fusion(f32[384,1152]{1,0:T(8,128)} %convolution_add_fusion.5, bf16[2,384,1152]{2,1,0:T(8,128)(2,1)} %collective-permute-done.1, f32[]{:T(128)} %bitcast.58, f32[]{:T(128)} %bitcast, bf16[384,1152]{1,0:T(8,128)(2,1)S(1)} %copy-done.2, f32[384]{0:T(512)S(1)} %add_rsqrt_fusion.1), kind=kOutput, calls=%fused_computation.8 | convolution fusion | flops 682131456 | bytes 6194696 | tf_op jit(solution)/shard_map/dot_general | solution.py:63
  56.7 4.8 %convolution_add_fusion.2 = f32[384,1152]{1,0:T(8,128)} fusion(f32[384,1152]{1,0:T(8,128)} %fusion.110, bf16[2,384,1152]{2,1,0:T(8,128)(2,1)} %collective-permute-done, f32[]{:T(128)} %bitcast.55, f32[]{:T(128)} %bitcast, bf16[384,1152]{1,0:T(8,128)(2,1)S(1)} %copy-done.1, f32[384]{0:T(512)S(1)} %add_rsqrt_fusion), kind=kOutput, calls=%fused_computation.4 | convolution fusion | flops 682131456 | bytes 6194696 | tf_op jit(solution)/shard_map/dot_general | solution.py:38
  61.5 4.8 %convolution_add_fusion.1 = f32[384,1152]{1,0:T(8,128)} fusion(f32[384,1152]{1,0:T(8,128)} %convolution_add_fusion.2, bf16[2,384,1152]{2,1,0:T(8,128)(2,1)} %collective-permute-done.1, f32[]{:T(128)} %bitcast.54, f32[]{:T(128)} %bitcast, bf16[384,1152]{1,0:T(8,128)(2,1)S(1)} %copy-done.1, f32[384]{0:T(512)S(1)} %add_rsqrt_fusion), kind=kOutput, calls=%fused_computation.3 | convolution fusion | flops 682131456 | bytes 6194696 | tf_op jit(solution)/shard_map/dot_general | solution.py:38
  66.3 4.2 %fusion.76 = f32[384,1152]{1,0:T(8,128)} fusion(bf16[2,384,1152]{2,1,0:T(8,128)(2,1)} %collective-permute-done.3, f32[]{:T(128)} %bitcast.52, f32[]{:T(128)} %bitcast, bf16[384,1152]{1,0:T(8,128)(2,1)S(1)} %copy-done.1, f32[384]{0:T(512)S(1)} %add_rsqrt_fusion), kind=kOutput, calls=%fused_computation.97 | convolution fusion | flops 681689088 | bytes 4425224 | tf_op jit(solution)/shard_map/dot_general | solution.py:38
  70.5 5.4 %fusion.15 = (f32[384]{0:T(512)S(1)}, f32[384,1152]{1,0:T(8,128)}) fusion(bf16[384,1152]{1,0:T(8,128)(2,1)S(1)} %copy-done.1, f32[384]{0:T(512)S(1)} %add_rsqrt_fusion, f32[384,1152]{1,0:T(8,128)} %fusion.76, f32[384,1152]{1,0:T(8,128)} %convolution_add_fusion.1, bf16[2,384,1152]{2,1,0:T(8,128)(2,1)} %collective-permute-done.2, f32[]{:T(128)} %bitcast.53, ...), kind=kOutput, calls=%fused_computation.25 | convolution fusion | flops 684785280 | bytes 8854528 | tf_op jit(solution)/shard_map/dot_general | solution.py:38
  76.0 1.9 fusion.18
  77.9 1.7 convolution_bitcast_fusion
  79.6 112.4 %all-reduce.1 = bf16[576,576]{0,1:T(8,128)(2,1)S(1)} all-reduce(f32[576,576]{0,1:T(8,128)} %convolution_bitcast_fusion), channel_id=1, replica_groups=mesh['dp'=512] {'dp'}, use_global_device_ids=true, to_apply=%region_4.0 | all-reduce | flops 331776 | bytes 1990656 | tf_op jit(solution)/shard_map/psum | solution.py:77
  192.0 1.2 copy.8
  193.2 4.0 %fusion.75 = f32[384,1152]{1,0:T(8,128)} fusion(bf16[2,384,1152]{2,1,0:T(8,128)(2,1)} %collective-permute-done.3, f32[]{:T(128)} %bitcast.56, f32[]{:T(128)} %bitcast, bf16[384,1152]{1,0:T(8,128)(2,1)S(1)} %copy-done.2, f32[384]{0:T(512)S(1)} %add_rsqrt_fusion.1), kind=kOutput, calls=%fused_computation.96 | convolution fusion | flops 681689088 | bytes 4425224 | tf_op jit(solution)/shard_map/dot_general | solution.py:63
  197.2 5.2 %fusion.10 = (f32[384]{0:T(512)S(1)}, f32[384,1152]{1,0:T(8,128)}) fusion(bf16[384,1152]{1,0:T(8,128)(2,1)S(1)} %copy-done.2, f32[384]{0:T(512)S(1)} %add_rsqrt_fusion.1, f32[384,1152]{1,0:T(8,128)} %fusion.75, f32[384,1152]{1,0:T(8,128)} %convolution_add_fusion.4, bf16[2,384,1152]{2,1,0:T(8,128)(2,1)} %collective-permute-done.2, f32[]{:T(128)} %bitcast.57, ...), kind=kOutput, calls=%fused_computation.20 | convolution fusion | flops 684785280 | bytes 8854528 | tf_op jit(solution)/shard_map/dot_general | solution.py:63
  202.4 2.8 %fusion.13 = bf16[384,1152]{1,0:T(8,128)(2,1)} fusion(f32[384,1152]{1,0:T(8,128)} %get-tuple-element.7, bf16[384,1152]{1,0:T(8,128)(2,1)S(1)} %copy-done.2, f32[384]{0:T(512)S(1)} %get-tuple-element.6, f32[384]{0:T(512)S(1)} %add_rsqrt_fusion.1), kind=kLoop, calls=%fused_computation.23 | loop fusion | flops 2654208 | bytes 3542016 | tf_op jit(solution)/shard_map/convert_element_type | solution.py:70
  (14 shorter events, 0.2 us)
Async XLA Ops:
  0.6 77.2 %copy-start = (bf16[384,576]{0,1:T(8,128)(2,1)S(1)}, bf16[384,576]{0,1:T(8,128)(2,1)}, u32[]{:S(2)}) copy-start(bf16[384,576]{0,1:T(8,128)(2,1)} %param.7) | copy-start | bytes 1327108
  0.6 3.0 %copy-start.2 = (bf16[384,1152]{1,0:T(8,128)(2,1)S(1)}, bf16[384,1152]{1,0:T(8,128)(2,1)}, u32[]{:S(2)}) copy-start(bf16[384,1152]{1,0:T(8,128)(2,1)} %param.5) | copy-start | bytes 2654212
  0.7 3.0 %copy-start.1 = (bf16[384,1152]{1,0:T(8,128)(2,1)S(1)}, bf16[384,1152]{1,0:T(8,128)(2,1)}, u32[]{:S(2)}) copy-start(bf16[384,1152]{1,0:T(8,128)(2,1)} %param.6) | copy-start | bytes 2654212
  4.2 24.0 %collective-permute-start.1 = (bf16[2,384,1152]{2,1,0:T(8,128)(2,1)S(1)}, bf16[2,384,1152]{2,1,0:T(8,128)(2,1)}, u32[]{:S(2)}, u32[]{:S(2)}) collective-permute-start(bf16[2,384,1152]{2,1,0:T(8,128)(2,1)S(1)} %pad_maximum_fusion), channel_id=1, source_target_pairs={{0,1},{1,2},{2,3},{3,4},{4,5},{5,6},{6,7},{7,8},{8,9},{9,10},{10,1... | collective-permute-start | bytes 5308424 | tf_op jit(solution)/shard_map/ppermute | solution.py:16
  8.9 26.0 %collective-permute-start = (bf16[2,384,1152]{2,1,0:T(8,128)(2,1)S(1)}, bf16[2,384,1152]{2,1,0:T(8,128)(2,1)}, u32[]{:S(2)}, u32[]{:S(2)}) collective-permute-start(bf16[2,384,1152]{2,1,0:T(8,128)(2,1)S(1)} %pad_maximum_fusion), channel_id=1, source_target_pairs={{0,511},{1,0},{2,1},{3,2},{4,3},{5,4},{6,5},{7,6},{8,7},{9,8},{10,... | collective-permute-start | bytes 5308424 | tf_op jit(solution)/shard_map/ppermute | solution.py:16
  28.3 38.0 %collective-permute-start.3 = (bf16[2,384,1152]{2,1,0:T(8,128)(2,1)}, bf16[2,384,1152]{2,1,0:T(8,128)(2,1)}, u32[]{:S(2)}, u32[]{:S(2)}) collective-permute-start(bf16[2,384,1152]{2,1,0:T(8,128)(2,1)} %collective-permute-done.1), channel_id=1, source_target_pairs={{0,1},{1,2},{2,3},{3,4},{4,5},{5,6},{6,7},{7,8},{8,9},{9,10},{10,1... | collective-permute-start | bytes 5308424 | tf_op jit(solution)/shard_map/ppermute | solution.py:16
  34.8 35.7 %collective-permute-start.2 = (bf16[2,384,1152]{2,1,0:T(8,128)(2,1)}, bf16[2,384,1152]{2,1,0:T(8,128)(2,1)}, u32[]{:S(2)}, u32[]{:S(2)}) collective-permute-start(bf16[2,384,1152]{2,1,0:T(8,128)(2,1)} %collective-permute-done), channel_id=1, source_target_pairs={{0,511},{1,0},{2,1},{3,2},{4,3},{5,4},{6,5},{7,6},{8,7},{9,8},{10,... | collective-permute-start | bytes 5308424 | tf_op jit(solution)/shard_map/ppermute | solution.py:16
  77.9 114.1 %copy-start.3 = (bf16[384,1152]{1,0:T(8,128)(2,1)}, bf16[384,1152]{1,0:T(8,128)(2,1)S(1)}, u32[]{:S(2)}) copy-start(bf16[384,1152]{1,0:T(8,128)(2,1)S(1)} %fusion.18) | copy-start | bytes 2654212
where the time goes:
time: 206 us; the launch traced here: 205 us
  blocking collectives  112 us (54%)
  matrix products  44.3 us (22%)
  starting transfers between devices  27.8 us (13%)
  waiting for transfers between devices  9.2 us (4%)
  other arithmetic  8.18 us (4%)
  between operations  2.1 us (1%)
    psum x1, blocking collectives, per_device(): head_grad = lax.psum(head_term, 'dp').astype(jnp.bfloat16)  112 us
    ppermute x4, starting transfers between devices, shifted(): return lax.ppermute(value, axis, pairs)  27.8 us
    dot_general x5, matrix products, column_sums(): lax.dot_general(tile_grad, rows_low, (((0,), (0,)), ((), ())), preferred_...  21.4 us
    dot_general x4, matrix products, per_device(): jnp.dot(tile_grad, nearby[0], preferred_element_type=jnp.float32)  18.4 us
    ppermute x4, waiting for transfers between devices, shifted(): return lax.ppermute(value, axis, pairs)  9.2 us
  transfers between devices with their start and end apart: 4, of which 1 were waited for; matrix products, arithmetic and copies ran while one was open for 14% of the time, Pallas kernels for 0%

commit v1 on v0

v1 whole, which is shorter than its diff:
```python
import functools

import jax
import jax.numpy as jnp
from jax import lax
from jax.experimental import pallas as pl
from jax.experimental.pallas import tpu as pltpu
from jax.sharding import PartitionSpec as P

D = 1152
HIN = 576
HOUT = 576
ROWS = 384
EPS = 1e-06

NX, NZ, NY = 4, 16, 4
CHIPS = NX * NZ * NY
NCH = 4
CH = ROWS // NCH
HALF = HIN // 2
WIDE = 640
PIECE = 336
OWNERS = 11
ZROWS = 32
PADDED = OWNERS * ZROWS

MESH = pl.DeviceIdType.MESH
BF16 = jnp.bfloat16
F32 = jnp.float32


def remote(src, dst, send, recv, device):
    return pltpu.make_async_remote_copy(
        src_ref=src, dst_ref=dst, send_sem=send, recv_sem=recv,
        device_id=(device,), device_id_type=MESH,
    )


def at(x, z, y, core):
    return ((x * NZ + z) * NY + y) * 2 + core


def kernel(
    image, text, text_in, log_scale, bias,
    image_grad, text_grad, head_grad,
    raw, inv, low, acc, far, near, grad, tin_t, tin_p, tg_p,
    hbuf, tail, xs, xr, red, zs, zr, ysum, yr, zg, hg, hout,
    in_sem, out_sem, leg_s, far_r, fwd_s, fwd_r, near_s, near_r,
    tin_s, tin_r, tg_s, tg_r, xs_s, xs_r, zs_s, zs_r, ys_s, ys_r,
    zg_s, zg_r, xg_s, xg_r, kg_s, kg_r,
):
    me = lax.axis_index("dp")
    core, chip = me % 2, me // 2
    y, z, x = chip % NY, (chip // NY) % NZ, chip // (NY * NZ)
    above, below = (chip + 1) % CHIPS, (chip + CHIPS - 1) % CHIPS
    other = 2 * chip + 1 - core
    giver = jnp.where(core == 0, 2 * below, 2 * above)
    to_up, to_down = 2 * above, 2 * below + 1
    x_peer = [at((x + j) % NX, z, y, core) for j in range(NX)]
    y_peer = [at(x, z, (y + j) % NY, core) for j in range(NY)]
    z_peer = [at(x, (z + j) % NZ, y, core) for j in range(NZ)]

    barrier = pltpu.get_barrier_semaphore()
    peers = [giver, giver + 1, other] + x_peer[1:] + y_peer[1:] + z_peer[1:]
    for peer in peers:
        pl.semaphore_signal(barrier, inc=1, device_id=(peer,), device_id_type=MESH)

    loads = [
        pltpu.make_async_copy(image, raw.at[0], in_sem.at[0]),
        pltpu.make_async_copy(text, raw.at[1], in_sem.at[1]),
        pltpu.make_async_copy(text_in, tin_t, in_sem.at[2]),
    ]
    for load in loads:
        load.start()

    scale = jnp.exp(jnp.full((8, 128), log_scale[0], F32))[0:1, 0:1]
    shift = jnp.full((8, 128), bias[0], F32)[0:1, 0:1]

    def normalize(side):
        def body(n, _):
            rows = pl.ds(pl.multiple_of(n * 16, 16), 16)
            wide = raw[side, rows, :].astype(F32)
            inverse = lax.rsqrt(jnp.sum(wide * wide, axis=-1, keepdims=True) + EPS)
            low[side, rows, :] = (wide * inverse).astype(BF16)
            inv[side, rows, :] = jnp.broadcast_to(inverse, (16, 128))
            return 0

        lax.fori_loop(0, ROWS // 16, body, 0, unroll=2)

    def part(n):
        return pl.ds(pl.multiple_of(n * CH, CH), CH)

    passed, kept = 1 - core, core

    def leg(side, up, n):
        return remote(
            low.at[side, part(n)], far.at[side, core, n],
            leg_s.at[side, up, n], far_r.at[side, core, n], to_up if up else to_down,
        )

    def arrived(side, slot, n):
        return remote(
            low.at[side, part(n)], far.at[side, slot, n],
            leg_s.at[side, 0, n], far_r.at[side, slot, n], to_up,
        )

    def own_over(side, n):
        return remote(
            low.at[side, part(n)], near.at[side, 0, n],
            near_s.at[side, n], near_r.at[side, n], other,
        )

    def pass_on(side, n):
        return remote(
            far.at[side, passed, n], near.at[side, 1, n],
            fwd_s.at[side, n], fwd_r.at[side, n], other,
        )

    def send_side(side):
        for n in range(NCH):
            leg(side, 0, n).start()
            leg(side, 1, n).start()
            own_over(side, n).start()

    def gate(left, right):
        dots = lax.dot_general(left, right, (((1,), (1,)), ((), ())), preferred_element_type=F32)
        return jax.nn.sigmoid(scale * dots + shift)

    def own_tile(side):
        rest = low[1 - side]
        mine = low[side]
        tile = gate(rest, mine)
        row = lax.broadcasted_iota(jnp.int32, (ROWS, ROWS), 0)
        col = lax.broadcasted_iota(jnp.int32, (ROWS, ROWS), 1)
        tile = (tile - jnp.where(row == col, 1.0, 0.0)).astype(BF16)
        acc[side] = jnp.dot(tile, mine, preferred_element_type=F32)

    def add_rows(side, rows):
        tile = gate(low[1 - side], rows).astype(BF16)
        acc[side] += jnp.dot(tile, rows, preferred_element_type=F32)

    def add_near(side):
        def body(n, _):
            own_over(side, n).wait_recv()
            add_rows(side, near[side, 0, n])
            return 0

        lax.fori_loop(0, NCH, body, 0)

    def add_far(side, n):
        arrived(side, passed, n).wait_recv()
        pass_on(side, n).start()
        add_rows(side, far[side, passed, n])
        arrived(side, kept, n).wait_recv()
        add_rows(side, far[side, kept, n])
        pass_on(side, n).wait_recv()
        add_rows(side, near[side, 1, n])

    def finish(side, n):
        for part_of in range(CH // 16):
            rows = pl.ds(pl.multiple_of(n * CH + part_of * 16, 16), 16)
            inverse = inv[1 - side, rows, 0:1]
            total = scale * acc[side, rows, :]
            unit = raw[1 - side, rows, :].astype(F32) * inverse
            along = jnp.sum(unit * total, axis=-1, keepdims=True)
            grad[side, rows, :] = ((total - unit * along) * inverse).astype(BF16)

    def out_copy(side, n):
        dst = (text_grad, image_grad)[side]
        return pltpu.make_async_copy(grad.at[side, part(n)], dst.at[part(n)], out_sem.at[side, n])

    loads[0].wait()
    normalize(0)
    pl.semaphore_wait(barrier, len(peers))
    send_side(0)
    loads[1].wait()
    normalize(1)
    send_side(1)
    own_tile(0)
    loads[2].wait()
    tin_copy = remote(
        tin_t.at[pl.ds(pl.multiple_of(HALF * (1 - core), HALF), HALF)], tin_p,
        tin_s.at[0], tin_r.at[0], other,
    )
    tin_copy.start()
    own_tile(1)
    add_near(0)
    add_near(1)

    def image_step(n, _):
        add_far(0, n)
        return 0

    lax.fori_loop(0, NCH, image_step, 0)

    def tg_copy(n):
        return remote(
            grad.at[0, part(n), pl.ds(0, WIDE)], tg_p.at[part(n)], tg_s.at[n], tg_r.at[n], other,
        )

    def finish_text(n, _):
        finish(0, n)
        tg_copy(n).start()
        out_copy(0, n).start()
        return 0

    lax.fori_loop(0, NCH, finish_text, 0)
    half = pl.ds(pl.multiple_of(HALF * core, HALF), HALF)
    hbuf[...] = jnp.dot(tin_t[half, :], grad[0, :, 0:WIDE], preferred_element_type=F32)
    tin_copy.wait_recv()
    for n in range(NCH):
        tg_copy(n).wait_recv()
    hbuf[...] += jnp.dot(tin_p[...], tg_p[...], preferred_element_type=F32)

    tail[0:144] = jnp.concatenate([hbuf[0:144, 512:576], hbuf[144:288, 512:576]], axis=1)
    tail[144:192] = jnp.zeros((48, 128), F32)
    for q in range(NX):
        xs[q, 0:HALF] = hbuf[:, 128 * q : 128 * q + 128].astype(BF16)
        xs[q, HALF:PIECE] = tail[48 * q : 48 * q + 48].astype(BF16)
    x_copy = [
        remote(xs.at[(x + j) % NX], xr.at[j - 1], xs_s.at[j - 1], xs_r.at[j - 1], x_peer[j])
        for j in range(1, NX)
    ]
    for copy in x_copy:
        copy.start()
    red[0:HALF] = hbuf[:, pl.ds(pl.multiple_of(128 * x, 128), 128)]
    red[HALF:PIECE] = tail[pl.ds(pl.multiple_of(48 * x, 16), 48)]
    red[PIECE:PADDED] = jnp.zeros((PADDED - PIECE, 128), F32)

    add_far(1, 0)

    for j in range(1, NX):
        x_copy[j - 1].wait_recv()
        red[0:PIECE] += xr[j - 1].astype(F32)
    zs[...] = red[...].astype(BF16)

    def share(pos):
        return (pos * OWNERS + NZ - 1) // NZ

    def owns(pos):
        return (share(pos) * NZ) // OWNERS == pos

    def rows_of(pos):
        return pl.ds(pl.multiple_of(ZROWS * share(pos), ZROWS), ZROWS)

    mine = owns(z)
    z_at = [(z + j) % NZ for j in range(NZ)]

    def z_copy(j):
        return remote(zs.at[rows_of(z_at[j])], zr.at[j - 1], zs_s.at[j - 1], zs_r.at[j - 1], z_peer[j])

    far_first = sorted(range(1, NZ), key=lambda j: -min(j, NZ - j))
    for j in far_first:
        @pl.when(owns(z_at[j]))
        def _():
            z_copy(j).start()

    def y_copy(j):
        return remote(ysum, yr.at[y], ys_s.at[j - 1], ys_r.at[j - 1], y_peer[j])

    def zg_copy(j):
        return remote(zg.at[rows_of(z)], zg.at[rows_of(z)], zg_s.at[j - 1], zg_r.at[j - 1], z_peer[j])

    @pl.when(mine)
    def _():
        total = red[rows_of(z), :]
        for j in range(1, NZ):
            remote(zs.at[0:ZROWS], zr.at[j - 1], zs_s.at[j - 1], zs_r.at[j - 1], z_peer[j]).wait_recv()
            total += zr[j - 1].astype(F32)
        ysum[...] = total
        for j in range(1, NY):
            y_copy(j).start()

    add_far(1, 1)

    @pl.when(mine)
    def _():
        yr[y] = ysum[...]
        for j in range(1, NY):
            y_copy(j).wait_recv()
        total = (yr[0] + yr[1]) + (yr[2] + yr[3])
        zg[rows_of(z), :] = total.astype(BF16)
        for j in far_first:
            zg_copy(j).start()

    add_far(1, 2)

    for j in range(1, NZ):
        source = (z - j + NZ) % NZ

        @pl.when(owns(source))
        def _():
            remote(
                zg.at[rows_of(source)], zg.at[rows_of(source)], zg_s.at[j - 1], zg_r.at[j - 1], z_peer[j]
            ).wait_recv()

    def xg_copy(j):
        return remote(zg.at[0:PIECE], hg.at[core, x], xg_s.at[j - 1], xg_r.at[j - 1], x_peer[j])

    def kg_copy(j):
        slot = hg.at[core, (x + j) % NX]
        return remote(slot, slot, kg_s.at[j], kg_r.at[j], other)

    for j in range(1, NX):
        xg_copy(j).start()
    hg[core, x] = zg[0:PIECE]
    kg_copy(0).start()

    add_far(1, 3)

    for j in range(1, NX):
        source = (x - j + NX) % NX
        remote(zg.at[0:PIECE], hg.at[core, source], xg_s.at[j - 1], xg_r.at[j - 1], x_peer[j]).wait_recv()
        kg_copy(NX - j).start()

    def finish_image(n, _):
        finish(1, n)
        out_copy(1, n).start()
        return 0

    lax.fori_loop(0, NCH, finish_image, 0)

    for j in range(NX):
        slot = hg.at[1 - core, (x + j) % NX]
        remote(slot, slot, kg_s.at[j], kg_r.at[j], other).wait_recv()
    for k in range(2):
        for q in range(NX):
            hout[HALF * k : HALF * k + HALF, 128 * q : 128 * q + 128] = hg[k, q, 0:HALF]
        for q in range(NX - 1):
            last = hg[k, q, HALF:PIECE]
            for h in range(2):
                first = HALF * k + 144 * h + 48 * q
                hout[first : first + 48, 512:576] = last[:, 64 * h : 64 * h + 64]
    head_copy = pltpu.make_async_copy(hout, head_grad, out_sem.at[2, 0])
    head_copy.start()

    for side in range(2):
        for n in range(NCH):
            leg(side, 0, n).wait_send()
            leg(side, 1, n).wait_send()
            own_over(side, n).wait_send()
            pass_on(side, n).wait_send()
    tin_copy.wait_send()
    for n in range(NCH):
        tg_copy(n).wait_send()
    for j in range(1, NX):
        x_copy[j - 1].wait_send()
        xg_copy(j).wait_send()
    for j in range(NX):
        kg_copy(j).wait_send()
    for j in range(1, NZ):
        @pl.when(owns(z_at[j]))
        def _():
            z_copy(j).wait_send()

    @pl.when(mine)
    def _():
        for j in range(1, NY):
            y_copy(j).wait_send()
        for j in range(1, NZ):
            zg_copy(j).wait_send()

    for side in range(2):
        for n in range(NCH):
            out_copy(side, n).wait()
    head_copy.wait()


def per_device(image, text, text_in, log_scale, bias):
    dma = pltpu.SemaphoreType.DMA
    vmem = pltpu.VMEM
    anywhere = pl.BlockSpec(memory_space=pl.ANY)
    scalars = pl.BlockSpec(memory_space=pltpu.SMEM)
    return pl.pallas_call(
        kernel,
        out_shape=(
            jax.ShapeDtypeStruct((ROWS, D), BF16),
            jax.ShapeDtypeStruct((ROWS, D), BF16),
            jax.ShapeDtypeStruct((HIN, HOUT), BF16),
        ),
        in_specs=[anywhere, anywhere, anywhere, scalars, scalars],
        out_specs=(anywhere, anywhere, anywhere),
        scratch_shapes=[
            vmem((2, ROWS, D), BF16),
            vmem((2, ROWS, 128), F32),
            vmem((2, ROWS, D), BF16),
            vmem((2, ROWS, D), F32),
            vmem((2, 2, NCH, CH, D), BF16),
            vmem((2, 2, NCH, CH, D), BF16),
            vmem((2, ROWS, D), BF16),
            vmem((HIN, ROWS), BF16),
            vmem((HALF, ROWS), BF16),
            vmem((ROWS, WIDE), BF16),
            vmem((HALF, WIDE), F32),
            vmem((192, 128), F32),
            vmem((NX, PIECE, 128), BF16),
            vmem((NX - 1, PIECE, 128), BF16),
            vmem((PADDED, 128), F32),
            vmem((PADDED, 128), BF16),
            vmem((NZ - 1, ZROWS, 128), BF16),
            vmem((ZROWS, 128), F32),
            vmem((NY, ZROWS, 128), F32),
            vmem((PADDED, 128), BF16),
            vmem((2, NX, PIECE, 128), BF16),
            vmem((HIN, HOUT), BF16),
            dma((3,)), dma((3, NCH)),
            dma((2, 2, NCH)), dma((2, 2, NCH)),
            dma((2, NCH)), dma((2, NCH)), dma((2, NCH)), dma((2, NCH)),
            dma((1,)), dma((1,)), dma((NCH,)), dma((NCH,)),
            dma((NX - 1,)), dma((NX - 1,)), dma((NZ - 1,)), dma((NZ - 1,)),
            dma((NY - 1,)), dma((NY - 1,)), dma((NZ - 1,)), dma((NZ - 1,)),
            dma((NX - 1,)), dma((NX - 1,)), dma((NX,)), dma((NX,)),
        ],
        compiler_params=pltpu.CompilerParams(
            collective_id=1, has_side_effects=True, vmem_limit_bytes=60 * 2**20
        ),
        cost_estimate=pl.CostEstimate(flops=7 * 10**9, bytes_accessed=5 * 10**6, transcendentals=2 * 10**6),
        name="band",
    )(image, text, text_in.T, log_scale, bias)


def solution(mesh):
    placed = (P("dp", None), P("dp", None), P("dp", None), P(), P())
    return jax.shard_map(
        per_device,
        mesh=mesh,
        in_specs=placed,
        out_specs=(P("dp", None), P("dp", None), P()),
        check_vma=False,
    )
```

time: 206 us -> 94.2 us (0.46)
  blocking collectives: 112 us -> 0 us
  Pallas kernels: 0 us -> 87.4 us
  matrix products: 44.3 us -> 0 us
  starting transfers between devices: 27.8 us -> 0 us
  waiting for transfers between devices: 9.2 us -> 0 us
  other arithmetic: 8.18 us -> 0 us
  local copies, waits for them, and re-layouts: 1.2 us -> 4.53 us
    psum x1 -> x0, blocking collectives: 112 us -> none  [per_device(): head_grad = lax.psum(head_term, 'dp').astype(jnp.bfloat16)]
    pallas_call x0 -> x1, Pallas kernels: none -> 87.4 us  [per_device(): pl.pallas_call(kernel, out_shape=(jax.ShapeDtypeStruct((ROWS, D), BF16),...]
    dot_general x12 -> x0, matrix products: 44.3 us -> none  [the longest x5 21.4 us: column_sums(): lax.dot_general(tile_grad, rows_low, (((0,), (0,)), ((), ())), preferred_...]
    ppermute x4 -> x0, starting transfers between devices: 27.8 us -> none  [shifted(): return lax.ppermute(value, axis, pairs)]
    ppermute x4 -> x0, waiting for transfers between devices: 9.2 us -> none  [shifted(): return lax.ppermute(value, axis, pairs)]
    convert_element_type x2 -> x0, other arithmetic: 4.63 us -> none  [the longest x1 2.77 us: per_device(): image_grad = ((grad_img - unit_img * jnp.sum(unit_img * grad_img, axis=-1...]
    unnamed x9 -> x7, local copies, waits for them, and re-layouts: 1.2 us -> 4.53 us
    reduce_sum x2 -> x0, other arithmetic: 2.99 us -> none  [unit_rows(): inverse = lax.rsqrt(jnp.sum(wide * wide, axis=-1, keepdims=True) + EPS)]
  transfers between devices with their start and end apart: 4 -> 0, of which waited for: 1 -> 0; matrix products, arithmetic and copies ran while one was open for 14% -> 0% of each run, Pallas kernels for 0% -> 0%
where the time goes in v1:
time: 94.2 us; the launch traced here: 93.9 us
  Pallas kernels  87.4 us (93%)
  local copies, waits for them, and re-layouts  4.53 us (5%)
  between operations  1.94 us (2%)
    pallas_call x1, Pallas kernels, per_device(): pl.pallas_call(kernel, out_shape=(jax.ShapeDtypeStruct((ROWS, D), BF16),...  87.4 us
    unnamed x7, local copies, waits for them, and re-layouts  4.53 us

profile of v1, /device:TPU:1, one launch (start us, length us, event | category | flops | bytes accessed | tf_op | source)
XLA Modules:
  0.0 93.9 jit_solution(17275688866584328037)
XLA Ops:
  1.9 87.4 %band.1 = (bf16[384,1152]{1,0:T(8,128)(2,1)}, bf16[384,1152]{1,0:T(8,128)(2,1)}, bf16[576,576]{1,0:T(8,128)(2,1)}) custom-call(bf16[384,1152]{1,0:T(8,128)(2,1)} %image.1, bf16[384,1152]{1,0:T(8,128)(2,1)} %text.1, bf16[576,384]{1,0:T(8,128)(2,1)} %bitcast.1, f32[1]{0:T(128)S(6)} %copy.11.log_scale, f32[1]{0:T(128)S(6)} %copy.12.bias), custom_call_target="tpu_custom_call" | custom-call | flops 7000000000 | bytes 5000000 | tf_op jit(solution)/shard_map/band/pallas_call | solution.py:374
  89.4 0.0 copy-start
  89.4 2.2 %copy.13 = bf16[384,1152]{1,0:T(8,128)(2,1)} copy(bf16[384,1152]{1,0:T(8,128)(2,1)} %get-tuple-element.6) | data formatting | bytes 1769472
  91.6 0.0 copy-done
  91.6 0.0 copy-start.1
  91.6 0.9 copy.14
  92.5 0.5 copy-done.1
  93.0 0.9 copy.15
Async XLA Ops:
  89.4 2.2 %copy-start = (bf16[384,1152]{1,0:T(8,128)(2,1)S(1)}, bf16[384,1152]{1,0:T(8,128)(2,1)}, u32[]{:S(2)}) copy-start(bf16[384,1152]{1,0:T(8,128)(2,1)} %get-tuple-element.7) | copy-start | bytes 2654212
  91.6 1.4 %copy-start.1 = (bf16[576,576]{1,0:T(8,128)(2,1)S(1)}, bf16[576,576]{1,0:T(8,128)(2,1)}, u32[]{:S(2)}) copy-start(bf16[576,576]{1,0:T(8,128)(2,1)} %get-tuple-element.8) | copy-start | bytes 1990660

commit v2 on v1

--- a/solution.py
+++ b/solution.py
@@ -23,6 +23,10 @@
 OWNERS = 11
 ZROWS = 32
 PADDED = OWNERS * ZROWS
+CUT = 192
+PARTS = ((0, CUT), (CUT, PIECE - CUT))
+
+SPLIT = 2
 
 MESH = pl.DeviceIdType.MESH
 BF16 = jnp.bfloat16
@@ -217,22 +221,21 @@
     for q in range(NX):
         xs[q, 0:HALF] = hbuf[:, 128 * q : 128 * q + 128].astype(BF16)
         xs[q, HALF:PIECE] = tail[48 * q : 48 * q + 48].astype(BF16)
-    x_copy = [
-        remote(xs.at[(x + j) % NX], xr.at[j - 1], xs_s.at[j - 1], xs_r.at[j - 1], x_peer[j])
-        for j in range(1, NX)
-    ]
-    for copy in x_copy:
-        copy.start()
+    def x_copy(h, j):
+        rows = pl.ds(*PARTS[h])
+        return remote(
+            xs.at[(x + j) % NX, rows], xr.at[j - 1, rows], xs_s.at[h, j - 1], xs_r.at[h, j - 1], x_peer[j]
+        )
+
+    for h in range(2):
+        for j in range(1, NX):
+            x_copy(h, j).start()
     red[0:HALF] = hbuf[:, pl.ds(pl.multiple_of(128 * x, 128), 128)]
     red[HALF:PIECE] = tail[pl.ds(pl.multiple_of(48 * x, 16), 48)]
     red[PIECE:PADDED] = jnp.zeros((PADDED - PIECE, 128), F32)
+    zs[PIECE:PADDED] = jnp.zeros((PADDED - PIECE, 128), BF16)
 
     add_far(1, 0)
-
-    for j in range(1, NX):
-        x_copy[j - 1].wait_recv()
-        red[0:PIECE] += xr[j - 1].astype(F32)
-    zs[...] = red[...].astype(BF16)
 
     def share(pos):
         return (pos * OWNERS + NZ - 1) // NZ
@@ -240,8 +243,12 @@
     def owns(pos):
         return (share(pos) * NZ) // OWNERS == pos
 
+    def owns_in(h, pos):
+        return jnp.logical_and(owns(pos), share(pos) % 2 == h)
+
     def rows_of(pos):
-        return pl.ds(pl.multiple_of(ZROWS * share(pos), ZROWS), ZROWS)
+        first = CUT * (share(pos) % 2) + ZROWS * (share(pos) // 2)
+        return pl.ds(pl.multiple_of(first, ZROWS), ZROWS)
 
     mine = owns(z)
     z_at = [(z + j) % NZ for j in range(NZ)]
@@ -250,10 +257,16 @@
         return remote(zs.at[rows_of(z_at[j])], zr.at[j - 1], zs_s.at[j - 1], zs_r.at[j - 1], z_peer[j])
 
     far_first = sorted(range(1, NZ), key=lambda j: -min(j, NZ - j))
-    for j in far_first:
-        @pl.when(owns(z_at[j]))
-        def _():
-            z_copy(j).start()
+    for h in range(2):
+        rows = pl.ds(*PARTS[h])
+        for j in range(1, NX):
+            x_copy(h, j).wait_recv()
+            red[rows] += xr[j - 1, rows].astype(F32)
+        zs[rows] = red[rows].astype(BF16)
+        for j in far_first:
+            @pl.when(owns_in(h, z_at[j]))
+            def _():
+                z_copy(j).start()
 
     def y_copy(j):
         return remote(ysum, yr.at[y], ys_s.at[j - 1], ys_r.at[j - 1], y_peer[j])
@@ -285,33 +298,46 @@
 
     add_far(1, 2)
 
-    for j in range(1, NZ):
-        source = (z - j + NZ) % NZ
-
-        @pl.when(owns(source))
-        def _():
-            remote(
-                zg.at[rows_of(source)], zg.at[rows_of(source)], zg_s.at[j - 1], zg_r.at[j - 1], z_peer[j]
-            ).wait_recv()
-
-    def xg_copy(j):
-        return remote(zg.at[0:PIECE], hg.at[core, x], xg_s.at[j - 1], xg_r.at[j - 1], x_peer[j])
-
-    def kg_copy(j):
-        slot = hg.at[core, (x + j) % NX]
-        return remote(slot, slot, kg_s.at[j], kg_r.at[j], other)
-
-    for j in range(1, NX):
-        xg_copy(j).start()
-    hg[core, x] = zg[0:PIECE]
-    kg_copy(0).start()
+    def xg_copy(h, j):
+        rows = pl.ds(*PARTS[h])
+        return remote(
+            zg.at[rows], hg.at[core, x, rows], xg_s.at[h, j - 1], xg_r.at[h, j - 1], x_peer[j]
+        )
+
+    def xg_wait(h, j):
+        rows = pl.ds(*PARTS[h])
+        source = (x - j + NX) % NX
+        remote(
+            zg.at[rows], hg.at[core, source, rows], xg_s.at[h, j - 1], xg_r.at[h, j - 1], x_peer[j]
+        ).wait_recv()
+
+    def kg_copy(h, j, side):
+        slot = hg.at[side, (x + j) % NX, pl.ds(*PARTS[h])]
+        return remote(slot, slot, kg_s.at[h, j], kg_r.at[h, j], other)
+
+    for h in range(2):
+        for j in range(1, NZ):
+            source = (z - j + NZ) % NZ
+
+            @pl.when(owns_in(h, source))
+            def _():
+                remote(
+                    zg.at[rows_of(source)], zg.at[rows_of(source)],
+                    zg_s.at[j - 1], zg_r.at[j - 1], z_peer[j],
+                ).wait_recv()
+
+        for j in range(1, NX):
+            xg_copy(h, j).start()
+        rows = pl.ds(*PARTS[h])
+        hg[core, x, rows] = zg[rows]
+        kg_copy(h, 0, core).start()
 
     add_far(1, 3)
 
-    for j in range(1, NX):
-        source = (x - j + NX) % NX
-        remote(zg.at[0:PIECE], hg.at[core, source], xg_s.at[j - 1], xg_r.at[j - 1], x_peer[j]).wait_recv()
-        kg_copy(NX - j).start()
+    for h in range(2):
+        for j in range(1, NX):
+            xg_wait(h, j)
+            kg_copy(h, NX - j, core).start()
 
     def finish_image(n, _):
         finish(1, n)
@@ -320,9 +346,9 @@
 
     lax.fori_loop(0, NCH, finish_image, 0)
 
-    for j in range(NX):
-        slot = hg.at[1 - core, (x + j) % NX]
-        remote(slot, slot, kg_s.at[j], kg_r.at[j], other).wait_recv()
+    for h in range(2):
+        for j in range(NX):
+            kg_copy(h, j, 1 - core).wait_recv()
     for k in range(2):
         for q in range(NX):
             hout[HALF * k : HALF * k + HALF, 128 * q : 128 * q + 128] = hg[k, q, 0:HALF]
@@ -343,11 +369,12 @@
     tin_copy.wait_send()
     for n in range(NCH):
         tg_copy(n).wait_send()
-    for j in range(1, NX):
-        x_copy[j - 1].wait_send()
-        xg_copy(j).wait_send()
-    for j in range(NX):
-        kg_copy(j).wait_send()
+    for h in range(2):
+        for j in range(1, NX):
+            x_copy(h, j).wait_send()
+            xg_copy(h, j).wait_send()
+        for j in range(NX):
+            kg_copy(h, j, core).wait_send()
     for j in range(1, NZ):
         @pl.when(owns(z_at[j]))
         def _():
@@ -366,12 +393,30 @@
     head_copy.wait()
 
 
+def hand_over(*refs):
+    sources, results, held, in_sems, out_sems = refs[:3], refs[3:6], refs[6:9], refs[9], refs[10]
+    reads, writes = [], []
+    for i, (src, dst, mid) in enumerate(zip(sources, results, held)):
+        rows = src.shape[0] // SPLIT
+        for n in range(SPLIT):
+            part = pl.ds(n * rows, rows)
+            reads.append(pltpu.make_async_copy(src.at[part], mid.at[part], in_sems.at[i, n]))
+            writes.append(pltpu.make_async_copy(mid.at[part], dst.at[part], out_sems.at[i, n]))
+    for read in reads:
+        read.start()
+    for read, write in zip(reads, writes):
+        read.wait()
+        write.start()
+    for write in writes:
+        write.wait()
+
+
 def per_device(image, text, text_in, log_scale, bias):
     dma = pltpu.SemaphoreType.DMA
     vmem = pltpu.VMEM
     anywhere = pl.BlockSpec(memory_space=pl.ANY)
     scalars = pl.BlockSpec(memory_space=pltpu.SMEM)
-    return pl.pallas_call(
+    grads = pl.pallas_call(
         kernel,
         out_shape=(
             jax.ShapeDtypeStruct((ROWS, D), BF16),
@@ -407,9 +452,9 @@
             dma((2, 2, NCH)), dma((2, 2, NCH)),
             dma((2, NCH)), dma((2, NCH)), dma((2, NCH)), dma((2, NCH)),
             dma((1,)), dma((1,)), dma((NCH,)), dma((NCH,)),
-            dma((NX - 1,)), dma((NX - 1,)), dma((NZ - 1,)), dma((NZ - 1,)),
+            dma((2, NX - 1)), dma((2, NX - 1)), dma((NZ - 1,)), dma((NZ - 1,)),
             dma((NY - 1,)), dma((NY - 1,)), dma((NZ - 1,)), dma((NZ - 1,)),
-            dma((NX - 1,)), dma((NX - 1,)), dma((NX,)), dma((NX,)),
+            dma((2, NX - 1)), dma((2, NX - 1)), dma((2, NX)), dma((2, NX)),
         ],
         compiler_params=pltpu.CompilerParams(
             collective_id=1, has_side_effects=True, vmem_limit_bytes=60 * 2**20
@@ -417,6 +462,15 @@
         cost_estimate=pl.CostEstimate(flops=7 * 10**9, bytes_accessed=5 * 10**6, transcendentals=2 * 10**6),
         name="band",
     )(image, text, text_in.T, log_scale, bias)
+    return pl.pallas_call(
+        hand_over,
+        out_shape=tuple(jax.ShapeDtypeStruct(g.shape, g.dtype) for g in grads),
+        in_specs=[anywhere] * 3,
+        out_specs=(anywhere,) * 3,
+        scratch_shapes=[vmem(g.shape, g.dtype) for g in grads] + [dma((3, SPLIT)), dma((3, SPLIT))],
+        cost_estimate=pl.CostEstimate(flops=0, bytes_accessed=5 * 10**6, transcendentals=0),
+        name="hand_over",
+    )(*grads)
 
 
 def solution(mesh):

time: 94.2 us -> 90.8 us (0.964)
  local copies, waits for them, and re-layouts: 4.53 us -> 0 us
  Pallas kernels: 87.4 us -> 88.6 us
    unnamed x7 -> x0, local copies, waits for them, and re-layouts: 4.53 us -> none
    pallas_call x0 -> x1, Pallas kernels: none -> 2.56 us  [per_device(): pl.pallas_call(hand_over, out_shape=tuple((jax.ShapeDtypeStruct(g.shape,...]
    pallas_call x1, Pallas kernels: 87.4 us -> 86 us  [per_device(): pl.pallas_call(kernel, out_shape=(jax.ShapeDtypeStruct((ROWS, D), BF16),...]
where the time goes in v2:
time: 90.8 us; the launch traced here: 90.7 us
  Pallas kernels  88.6 us (98%)
  between operations  2.09 us (2%)
    pallas_call x1, Pallas kernels, per_device(): pl.pallas_call(kernel, out_shape=(jax.ShapeDtypeStruct((ROWS, D), BF16),...  86 us
    pallas_call x1, Pallas kernels, per_device(): pl.pallas_call(hand_over, out_shape=tuple((jax.ShapeDtypeStruct(g.shape,...  2.56 us

profile of v2, /device:TPU:1, one launch (start us, length us, event | category | flops | bytes accessed | tf_op | source)
XLA Modules:
  0.0 90.7 jit_solution(17487888041910455304)
XLA Ops:
  1.9 86.0 %band.1 = (bf16[384,1152]{1,0:T(8,128)(2,1)}, bf16[384,1152]{1,0:T(8,128)(2,1)}, bf16[576,576]{1,0:T(8,128)(2,1)}) custom-call(bf16[384,1152]{1,0:T(8,128)(2,1)} %image.1, bf16[384,1152]{1,0:T(8,128)(2,1)} %text.1, bf16[576,384]{1,0:T(8,128)(2,1)} %bitcast.1, f32[1]{0:T(128)S(6)} %copy.8.log_scale, f32[1]{0:T(128)S(6)} %copy.9.bias), custom_call_target="tpu_custom_call" | custom-call | flops 7000000000 | bytes 5000000 | tf_op jit(solution)/shard_map/band/pallas_call | solution.py:419
  87.9 2.6 %hand_over.1 = (bf16[384,1152]{1,0:T(8,128)(2,1)}, bf16[384,1152]{1,0:T(8,128)(2,1)}, bf16[576,576]{1,0:T(8,128)(2,1)}) custom-call(bf16[384,1152]{1,0:T(8,128)(2,1)} %get-tuple-element.6.refs_0_, bf16[384,1152]{1,0:T(8,128)(2,1)} %get-tuple-element.7.refs_1_, bf16[576,576]{1,0:T(8,128)(2,1)} %get-tuple-element.8.refs_2_), custom_call_target="tpu_custom_call" | custom-call | bytes 5000000 | tf_op jit(solution)/shard_map/hand_over/pallas_call | solution.py:465

commit v3 on v2

--- a/solution.py
+++ b/solution.py
@@ -334,17 +334,17 @@
 
     add_far(1, 3)
 
-    for h in range(2):
-        for j in range(1, NX):
-            xg_wait(h, j)
-            kg_copy(h, NX - j, core).start()
-
     def finish_image(n, _):
         finish(1, n)
         out_copy(1, n).start()
         return 0
 
     lax.fori_loop(0, NCH, finish_image, 0)
+
+    for h in range(2):
+        for j in range(1, NX):
+            xg_wait(h, j)
+            kg_copy(h, NX - j, core).start()
 
     for h in range(2):
         for j in range(NX):

time: 90.8 us -> 91 us (level)
  no operation moved by 1% of the time
where the time goes in v3:
time: 91 us; the launch traced here: 90.8 us
  Pallas kernels  88.7 us (97%)
  between operations  2.09 us (2%)
    pallas_call x1, Pallas kernels, per_device(): pl.pallas_call(kernel, out_shape=(jax.ShapeDtypeStruct((ROWS, D), BF16),...  86.1 us
    pallas_call x1, Pallas kernels, per_device(): pl.pallas_call(hand_over, out_shape=tuple((jax.ShapeDtypeStruct(g.shape,...  2.56 us

profile of v3, /device:TPU:1, one launch (start us, length us, event | category | flops | bytes accessed | tf_op | source)
XLA Modules:
  0.0 90.8 jit_solution(4174428113975641752)
XLA Ops:
  1.9 86.1 %band.1 = (bf16[384,1152]{1,0:T(8,128)(2,1)}, bf16[384,1152]{1,0:T(8,128)(2,1)}, bf16[576,576]{1,0:T(8,128)(2,1)}) custom-call(bf16[384,1152]{1,0:T(8,128)(2,1)} %image.1, bf16[384,1152]{1,0:T(8,128)(2,1)} %text.1, bf16[576,384]{1,0:T(8,128)(2,1)} %bitcast.1, f32[1]{0:T(128)S(6)} %copy.8.log_scale, f32[1]{0:T(128)S(6)} %copy.9.bias), custom_call_target="tpu_custom_call" | custom-call | flops 7000000000 | bytes 5000000 | tf_op jit(solution)/shard_map/band/pallas_call | solution.py:419
  88.0 2.6 %hand_over.1 = (bf16[384,1152]{1,0:T(8,128)(2,1)}, bf16[384,1152]{1,0:T(8,128)(2,1)}, bf16[576,576]{1,0:T(8,128)(2,1)}) custom-call(bf16[384,1152]{1,0:T(8,128)(2,1)} %get-tuple-element.6.refs_0_, bf16[384,1152]{1,0:T(8,128)(2,1)} %get-tuple-element.7.refs_1_, bf16[576,576]{1,0:T(8,128)(2,1)} %get-tuple-element.8.refs_2_), custom_call_target="tpu_custom_call" | custom-call | bytes 5000000 | tf_op jit(solution)/shard_map/hand_over/pallas_call | solution.py:465
